TPU v7x, 256 devices: a whole 4x4x8 slice. The times are simulated.
256 devices in a mesh: dp: 8 (over x, core), clus: 32 (over z, y).
Axes of the slice: x: 4, y: 4, z: 8, core: 2. Of those that a mesh axis runs over, the one named last changes fastest.
Arguments:
- activations: bfloat16 [1024, 12288], P('clus', 'dp'), may hold values from -6 to 6
- picks: int32 [1024, 48], replicated, may hold values from 0 to 383, all different within a row
- up_weight: bfloat16 [384, 12288, 128], P('clus', 'dp'), may hold values from -0.0546875 to 0.0546875
- up_bias: float32 [384, 128], P('clus'), may hold values from -3 to 3
- down_weight: bfloat16 [384, 128, 12288], P('clus', None, 'dp'), may hold values from -0.078125 to 0.078125
Outputs:
- layer_out: bfloat16 [1024, 12288], P('clus', 'dp')
Inputs may be any that keep to these rules, and one draw needn't show every extreme that they name: `picks`: each row names 48 distinct clusters; every cluster is named by some row.
All inputs are finite; a program needn't handle non-finite values.
Results may differ from a plain program's by a relative error of at most 0.012.
Values may be sent and summed in bfloat16 or wider, within the bound.
No kernel may reach another device: no remote copies, remote signals or barrier semaphores. Data moves between devices by JAX's collectives and lax.ppermute only.
A program may use at most 64 MiB of HBM per device.

v0:
```python
import jax
import jax.numpy as jnp
from jax import lax
from jax.sharding import PartitionSpec as P


def on_device(activations, picks, up_weight, up_bias, down_weight):
    tok_rows = activations.shape[0]
    clusters_here = up_weight.shape[0]
    ngroups = lax.axis_size("clus")
    own_index = lax.axis_index("clus")
    wanted = own_index * clusters_here + jnp.arange(clusters_here, dtype=jnp.int32)
    cluster_mask = jnp.any(picks[:, :, None] == wanted[None, None, :], axis=1).astype(jnp.float32)
    partial_pre = jnp.einsum(
        "rd,cdn->rcn",
        lax.all_gather(activations, "clus", axis=0, tiled=True),
        up_weight,
        preferred_element_type=jnp.float32,
    )
    summed = lax.psum(partial_pre, "dp")
    hidden = (jnp.maximum(summed + up_bias[None], 0.0) * cluster_mask[:, :, None]).astype(
        jnp.bfloat16
    )
    produced = jnp.einsum(
        "rcn,cnd->rd", hidden, down_weight, preferred_element_type=jnp.float32
    ).astype(jnp.bfloat16)
    returned = lax.all_to_all(produced, "clus", split_axis=0, concat_axis=0, tiled=True)
    combined = jnp.sum(returned.reshape(ngroups, tok_rows, -1).astype(jnp.float32), axis=0)
    return combined.astype(jnp.bfloat16)


def solution(mesh):
    placed = (P("clus", "dp"), P(), P("clus", "dp", None), P("clus", None), P("clus", None, "dp"))
    return jax.shard_map(
        on_device, mesh=mesh, in_specs=placed, out_specs=P("clus", "dp"), check_vma=False
    )
```

profile of v0, /device:TPU:19, one launch (start us, length us, event | category | flops | bytes accessed | tf_op | source)
XLA Modules:
  0.0 287.9 jit_solution(2460039226780015000)
XLA Ops:
  6.5 0.0 all-gather.2.cloned.1.call-start
  6.5 0.7 all-gather.2.cloned.1.call-update
  7.3 0.0 all-reduce.2.cloned.1.call-start
  7.3 80.6 %all-gather.2.cloned.1.call-done = bf16[1024,1536]{1,0:T(8,128)(2,1)} async-done(((bf16[32,1536]{1,0:T(8,128)(2,1)}), bf16[1024,1536]{1,0:T(8,128)(2,1)}) %all-gather.2.cloned.1.call-update) | async-done | bytes 3145744 | tf_op jit(solution)/shard_map/all_gather | solution.py:16
  87.9 9.7 %fusion = f32[1024,12,128]{2,0,1:T(8,128)} fusion(bf16[12,1536,128]{2,1,0:T(8,128)(2,1)} %param.7, bf16[1024,1536]{1,0:T(8,128)(2,1)} %all-gather.2.cloned.1.call-done), kind=kOutput, calls=%fused_computation.2 | convolution fusion | flops 4831838208 | bytes 14155776 | tf_op jit(solution)/shard_map/rd,cdn->rcn/dot_general | solution.py:14
  97.6 0.0 copy-start
  97.6 0.0 copy-start.1
  97.6 0.0 all-reduce.2.cloned.1.call-update
  97.7 0.9 copy-done
  98.5 0.4 compare_reduce_fusion
  99.0 88.9 %all-reduce.2.cloned.1.call-done = f32[1024,12,128]{2,0,1:T(8,128)} async-done(((f32[1024,12,128]{2,0,1:T(8,128)}), f32[1024,12,128]{2,0,1:T(8,128)}) %all-reduce.2.cloned.1.call-update) | async-done | bytes 6291472 | tf_op jit(solution)/shard_map/psum | solution.py:20
  187.9 0.0 copy-done.1
  187.9 8.6 %bitcast_convert_fusion = bf16[1024,1536]{1,0:T(8,128)(2,1)S(1)} fusion(bf16[12,128,1536]{2,1,0:T(8,128)(2,1)} %param.9, f32[1024,12,128]{2,0,1:T(8,128)} %all-reduce.2.cloned.1.call-done, f32[1024,12]{0,1:T(8,128)S(1)} %convert_element_type.15, f32[12,128]{1,0:T(8,128)S(1)} %copy-done.1), kind=kOutput, calls=%fused_computation | convolution fusion | flops 4839702528 | bytes 14211072 | tf_op jit(solution)/shard_map/rcn,cnd->rd/dot_general | solution.py:24
  196.5 83.4 %all_to_all.9 = bf16[32,32,1536]{2,1,0:T(8,128)(2,1)S(1)} all-to-all(bf16[32,32,1536]{2,1,0:T(8,128)(2,1)S(1)} %bitcast.8), channel_id=1, replica_groups=mesh['dp'=8,'clus'=32] {'clus'}, dimensions={0} | all-to-all | bytes 6291456 | tf_op jit(solution)/shard_map/all_to_all | solution.py:27
  279.9 1.1 reduce_sum.12
  (2 shorter events, 0.0 us)
Async XLA Ops:
  6.5 81.4 %all-gather.2.cloned.1.call-start = ((), (), s32[]{:S(2)}) async-start(), calls=%async_computation.1 | async-start | bytes 3244032 | tf_op jit(solution)/shard_map/all_gather | solution.py:16
  7.3 180.6 %all-reduce.2.cloned.1.call-start = ((), (), s32[]{:S(2)}) async-start(), calls=%async_computation.2 | async-start | bytes 12582912 | tf_op jit(solution)/shard_map/psum | solution.py:20
  97.6 0.9 copy-start
  97.6 90.2 %copy-start.1 = (f32[12,128]{1,0:T(8,128)S(1)}, f32[12,128]{1,0:T(8,128)}, u32[]{:S(2)}) copy-start(f32[12,128]{1,0:T(8,128)} %param.8) | copy-start | bytes 18436
Sparse Core Ops, SparseCore 0:
  9.9 77.9 all-gather.1
  97.8 90.0 all-reduce.1
where the time goes:
time: 288 us
  waiting for transfers between devices  170 us (59%)
  blocking collectives  83.4 us (29%)
  matrix products  18.4 us (6%)
  between operations  13.4 us (5%)
    psum x1, waiting for transfers between devices, on_device(): summed = lax.psum(partial_pre, 'dp')  88.9 us
    all_to_all x1, blocking collectives, on_device(): lax.all_to_all(produced, 'clus', split_axis=0, concat_axis=0, tiled=True)  83.4 us
    all_gather x1, waiting for transfers between devices, on_device(): lax.all_gather(activations, 'clus', axis=0, tiled=True)  80.6 us
    dot_general x1, matrix products, on_device(): jnp.einsum('rd,cdn->rcn', lax.all_gather(activations, 'clus', axis=0, til...  9.73 us
    dot_general x1, matrix products, on_device(): jnp.einsum('rcn,cnd->rd', hidden, down_weight, preferred_element_type=jnp...  8.65 us
  transfers between devices with their start and end apart: 2, of which 2 were waited for; matrix products, arithmetic and copies ran while one was open for 0% of the time, Pallas kernels for 0%

commit v1 on v0

--- a/solution.py
+++ b/solution.py
@@ -2,6 +2,18 @@
 import jax.numpy as jnp
 from jax import lax
 from jax.sharding import PartitionSpec as P
+
+
+def gather_by_bits(x, axis, dim):
+    ways, here, lap = (lax.axis_size(axis), lax.axis_index(axis), x.shape[dim])
+    line, have = (x, 1)
+    while have < ways:
+        line = jnp.concatenate(
+            [line, lax.ppermute(line, axis, [(d, (d - have) % ways) for d in range(ways)])],
+            axis=dim,
+        )
+        have = 2 * have
+    return jnp.roll(line, here * lap, axis=dim)
 
 
 def on_device(activations, picks, up_weight, up_bias, down_weight):
@@ -13,7 +25,7 @@
     cluster_mask = jnp.any(picks[:, :, None] == wanted[None, None, :], axis=1).astype(jnp.float32)
     partial_pre = jnp.einsum(
         "rd,cdn->rcn",
-        lax.all_gather(activations, "clus", axis=0, tiled=True),
+        gather_by_bits(activations, "clus", 0),
         up_weight,
         preferred_element_type=jnp.float32,
     )

time: 288 us -> 350 us (1.22)
  waiting for transfers between devices: 170 us -> 202 us
  starting transfers between devices: 0.04 us -> 16 us
  local copies, waits for them, and re-layouts: 0.89 us -> 12.4 us
    ppermute x0 -> x5, waiting for transfers between devices: none -> 97.4 us  [gather_by_bits(): lax.ppermute(line, axis, [(d, (d - have) % ways) for d in range(ways)])]
    all_gather x1 -> x0, waiting for transfers between devices: 80.6 us -> none  [on_device(): lax.all_gather(activations, 'clus', axis=0, tiled=True)]
    psum x1, waiting for transfers between devices: 88.9 us -> 105 us  [on_device(): summed = lax.psum(partial_pre, 'dp')]
    ppermute x0 -> x5, starting transfers between devices: none -> 16 us  [gather_by_bits(): lax.ppermute(line, axis, [(d, (d - have) % ways) for d in range(ways)])]
    unnamed x4 -> x16, local copies, waits for them, and re-layouts: 0.89 us -> 9.85 us
  transfers between devices with their start and end apart: 2 -> 6, of which waited for: 2 -> 6; matrix products, arithmetic and copies ran while one was open for 0% -> 1% of each run, Pallas kernels for 0% -> 0%
where the time goes in v1:
time: 350 us
  waiting for transfers between devices  202 us (58%)
  blocking collectives  83.4 us (24%)
  matrix products  18.3 us (5%)
  starting transfers between devices  16 us (5%)
  between operations  13.4 us (4%)
  local copies, waits for them, and re-layouts  12.4 us (4%)
  other arithmetic  4.27 us (1%)
    psum x1, waiting for transfers between devices, on_device(): summed = lax.psum(partial_pre, 'dp')  105 us
    ppermute x5, waiting for transfers between devices, gather_by_bits(): lax.ppermute(line, axis, [(d, (d - have) % ways) for d in range(ways)])  97.4 us
    all_to_all x1, blocking collectives, on_device(): lax.all_to_all(produced, 'clus', split_axis=0, concat_axis=0, tiled=True)  83.4 us
    ppermute x5, starting transfers between devices, gather_by_bits(): lax.ppermute(line, axis, [(d, (d - have) % ways) for d in range(ways)])  16 us
    unnamed x16, local copies, waits for them, and re-layouts  9.85 us
    dot_general x1, matrix products, on_device(): jnp.einsum('rd,cdn->rcn', gather_by_bits(activations, 'clus', 0), up_weig...  9.69 us
    dot_general x1, matrix products, on_device(): jnp.einsum('rcn,cnd->rd', hidden, down_weight, preferred_element_type=jnp...  8.66 us
  transfers between devices with their start and end apart: 6, of which 6 were waited for; matrix products, arithmetic and copies ran while one was open for 1% of the time, Pallas kernels for 0%

profile of v1, /device:TPU:19, one launch (start us, length us, event | category | flops | bytes accessed | tf_op | source)
XLA Modules:
  0.0 350.2 jit_solution(11598879983751627764)
XLA Ops:
  6.5 0.0 copy-start
  6.5 0.0 all-reduce.2.cloned.1.call-start
  6.5 0.2 collective-permute-start
  6.7 3.5 %collective-permute-done = bf16[32,1536]{1,0:T(8,128)(2,1)S(1)} collective-permute-done((bf16[32,1536]{1,0:T(8,128)(2,1)}, bf16[32,1536]{1,0:T(8,128)(2,1)S(1)}, u32[]{:S(2)}, u32[]{:S(2)}) %collective-permute-start) | collective-permute-done | bytes 98336 | tf_op jit(solution)/shard_map/ppermute | solution.py:12
  10.2 0.9 pad_maximum_fusion.2
  11.1 6.4 %collective-permute-start.1 = (bf16[64,1536]{1,0:T(8,128)(2,1)S(1)}, bf16[64,1536]{1,0:T(8,128)(2,1)S(1)}, u32[]{:S(2)}, u32[]{:S(2)}) collective-permute-start(bf16[64,1536]{1,0:T(8,128)(2,1)S(1)} %pad_maximum_fusion.2), channel_id=1, source_target_pairs={{0,30},{1,31},{2,0},{3,1},{4,2},{5,3},{6,4},{7,5},{8,6},{9,7},{10,... | collective-permute-start | bytes 589832 | tf_op jit(solution)/shard_map/ppermute | solution.py:12
  17.6 2.6 collective-permute-done.1
  20.2 0.9 pad_maximum_fusion.1
  21.1 4.8 %collective-permute-start.2 = (bf16[128,1536]{1,0:T(8,128)(2,1)S(1)}, bf16[128,1536]{1,0:T(8,128)(2,1)S(1)}, u32[]{:S(2)}, u32[]{:S(2)}) collective-permute-start(bf16[128,1536]{1,0:T(8,128)(2,1)S(1)} %pad_maximum_fusion.1), channel_id=1, source_target_pairs={{0,28},{1,29},{2,30},{3,31},{4,0},{5,1},{6,2},{7,3},{8,4},{9,5},{1... | collective-permute-start | bytes 1179656 | tf_op jit(solution)/shard_map/ppermute | solution.py:12
  25.9 5.4 %collective-permute-done.2 = bf16[128,1536]{1,0:T(8,128)(2,1)S(1)} collective-permute-done((bf16[128,1536]{1,0:T(8,128)(2,1)S(1)}, bf16[128,1536]{1,0:T(8,128)(2,1)S(1)}, u32[]{:S(2)}, u32[]{:S(2)}) %collective-permute-start.2) | collective-permute-done | bytes 393248 | tf_op jit(solution)/shard_map/ppermute | solution.py:12
  31.3 0.9 pad_maximum_fusion
  32.3 2.3 collective-permute-start.3
  34.6 1.6 constant_dynamic-update-slice_fusion.4
  36.2 0.7 constant_dynamic-update-slice_fusion.3
  36.8 0.8 constant_dynamic-update-slice_fusion.2
  37.6 1.0 constant_dynamic-update-slice_fusion.1
  38.6 16.2 %collective-permute-done.3 = bf16[256,1536]{1,0:T(8,128)(2,1)S(1)} collective-permute-done((bf16[256,1536]{1,0:T(8,128)(2,1)S(1)}, bf16[256,1536]{1,0:T(8,128)(2,1)S(1)}, u32[]{:S(2)}, u32[]{:S(2)}) %collective-permute-start.3) | collective-permute-done | bytes 786464 | tf_op jit(solution)/shard_map/ppermute | solution.py:12
  54.8 1.3 constant_dynamic-update-slice_fusion
  56.1 2.3 collective-permute-start.4
  58.4 69.6 %collective-permute-done.4 = bf16[512,1536]{1,0:T(8,128)(2,1)S(1)} collective-permute-done((bf16[512,1536]{1,0:T(8,128)(2,1)}, bf16[512,1536]{1,0:T(8,128)(2,1)S(1)}, u32[]{:S(2)}, u32[]{:S(2)}) %collective-permute-start.4) | collective-permute-done | bytes 1572896 | tf_op jit(solution)/shard_map/ppermute | solution.py:12
  128.0 1.3 constant_dynamic-update-slice_fusion.11
  129.3 0.0 copy-done
  129.3 0.6 constant_dynamic-update-slice_fusion.10
  129.9 0.6 constant_dynamic-update-slice_fusion.9
  130.6 0.7 constant_dynamic-update-slice_fusion.8
  131.3 0.8 constant_dynamic-update-slice_fusion.7
  132.0 0.9 constant_dynamic-update-slice_fusion.6
  133.0 1.3 constant_dynamic-update-slice_fusion.5
  134.2 9.7 %fusion = f32[1024,12,128]{2,0,1:T(8,128)} fusion(bf16[12,1536,128]{2,1,0:T(8,128)(2,1)} %param.7, bf16[2048,1536]{1,0:T(8,128)(2,1)} %constant_dynamic-update-slice_fusion.5, s32[]{:T(128)S(6)} %select_n.14), kind=kOutput, calls=%fused_computation.2 | convolution fusion | flops 4831838208 | bytes 14155780 | tf_op jit(solution)/shard_map/rd,cdn->rcn/dot_general | solution.py:26
  143.9 0.0 copy-start.1
  143.9 0.0 copy-start.2
  143.9 0.0 all-reduce.2.cloned.1.call-update
  144.0 0.9 copy-done.1
  144.9 0.4 compare_reduce_fusion
  145.3 104.9 %all-reduce.2.cloned.1.call-done = f32[1024,12,128]{2,0,1:T(8,128)} async-done(((f32[1024,12,128]{2,0,1:T(8,128)}), f32[1024,12,128]{2,0,1:T(8,128)}) %all-reduce.2.cloned.1.call-update) | async-done | bytes 6291472 | tf_op jit(solution)/shard_map/psum | solution.py:32
  250.2 0.0 copy-done.2
  250.2 8.7 %bitcast_convert_fusion = bf16[1024,1536]{1,0:T(8,128)(2,1)S(1)} fusion(bf16[12,128,1536]{2,1,0:T(8,128)(2,1)} %param.9, f32[1024,12,128]{2,0,1:T(8,128)} %all-reduce.2.cloned.1.call-done, f32[1024,12]{0,1:T(8,128)S(1)} %convert_element_type.15, f32[12,128]{1,0:T(8,128)S(1)} %copy-done.2), kind=kOutput, calls=%fused_computation | convolution fusion | flops 4839702528 | bytes 14211072 | tf_op jit(solution)/shard_map/rcn,cnd->rd/dot_general | solution.py:36
  258.9 83.4 %all_to_all.9 = bf16[32,32,1536]{2,1,0:T(8,128)(2,1)S(1)} all-to-all(bf16[32,32,1536]{2,1,0:T(8,128)(2,1)S(1)} %bitcast.8), channel_id=1, replica_groups=mesh['dp'=8,'clus'=32] {'clus'}, dimensions={0} | all-to-all | bytes 6291456 | tf_op jit(solution)/shard_map/all_to_all | solution.py:39
  342.3 1.1 reduce_sum.12
  (2 shorter events, 0.0 us)
Async XLA Ops:
  6.5 122.8 %copy-start = (bf16[32,1536]{1,0:T(8,128)(2,1)S(1)}, bf16[32,1536]{1,0:T(8,128)(2,1)}, u32[]{:S(2)}) copy-start(bf16[32,1536]{1,0:T(8,128)(2,1)} %param.5) | copy-start | bytes 294916
  6.5 243.7 %all-reduce.2.cloned.1.call-start = ((), (), s32[]{:S(2)}) async-start(), calls=%async_computation.1 | async-start | bytes 12582912 | tf_op jit(solution)/shard_map/psum | solution.py:32
  6.5 3.7 %collective-permute-start = (bf16[32,1536]{1,0:T(8,128)(2,1)}, bf16[32,1536]{1,0:T(8,128)(2,1)S(1)}, u32[]{:S(2)}, u32[]{:S(2)}) collective-permute-start(bf16[32,1536]{1,0:T(8,128)(2,1)} %param.5), channel_id=1, source_target_pairs={{0,31},{1,0},{2,1},{3,2},{4,3},{5,4},{6,5},{7,6},{8,7},{9,8},{10,9... | collective-permute-start | bytes 294920 | tf_op jit(solution)/shard_map/ppermute | solution.py:12
  11.1 9.1 %collective-permute-start.1 = (bf16[64,1536]{1,0:T(8,128)(2,1)S(1)}, bf16[64,1536]{1,0:T(8,128)(2,1)S(1)}, u32[]{:S(2)}, u32[]{:S(2)}) collective-permute-start(bf16[64,1536]{1,0:T(8,128)(2,1)S(1)} %pad_maximum_fusion.2), channel_id=1, source_target_pairs={{0,30},{1,31},{2,0},{3,1},{4,2},{5,3},{6,4},{7,5},{8,6},{9,7},{10,... | collective-permute-start | bytes 589832 | tf_op jit(solution)/shard_map/ppermute | solution.py:12
  21.1 10.2 %collective-permute-start.2 = (bf16[128,1536]{1,0:T(8,128)(2,1)S(1)}, bf16[128,1536]{1,0:T(8,128)(2,1)S(1)}, u32[]{:S(2)}, u32[]{:S(2)}) collective-permute-start(bf16[128,1536]{1,0:T(8,128)(2,1)S(1)} %pad_maximum_fusion.1), channel_id=1, source_target_pairs={{0,28},{1,29},{2,30},{3,31},{4,0},{5,1},{6,2},{7,3},{8,4},{9,5},{1... | collective-permute-start | bytes 1179656 | tf_op jit(solution)/shard_map/ppermute | solution.py:12
  32.3 22.5 %collective-permute-start.3 = (bf16[256,1536]{1,0:T(8,128)(2,1)S(1)}, bf16[256,1536]{1,0:T(8,128)(2,1)S(1)}, u32[]{:S(2)}, u32[]{:S(2)}) collective-permute-start(bf16[256,1536]{1,0:T(8,128)(2,1)S(1)} %pad_maximum_fusion), channel_id=1, source_target_pairs={{0,24},{1,25},{2,26},{3,27},{4,28},{5,29},{6,30},{7,31},{8,0},{9,1... | collective-permute-start | bytes 2359304 | tf_op jit(solution)/shard_map/ppermute | solution.py:12
  56.1 71.9 %collective-permute-start.4 = (bf16[512,1536]{1,0:T(8,128)(2,1)}, bf16[512,1536]{1,0:T(8,128)(2,1)S(1)}, u32[]{:S(2)}, u32[]{:S(2)}) collective-permute-start(bf16[512,1536]{1,0:T(8,128)(2,1)} %get-tuple-element.5), channel_id=1, source_target_pairs={{0,16},{1,17},{2,18},{3,19},{4,20},{5,21},{6,22},{7,23},{8,24},{9,... | collective-permute-start | bytes 4718600 | tf_op jit(solution)/shard_map/ppermute | solution.py:12
  143.9 0.9 copy-start.1
  143.9 106.3 %copy-start.2 = (f32[12,128]{1,0:T(8,128)S(1)}, f32[12,128]{1,0:T(8,128)}, u32[]{:S(2)}) copy-start(f32[12,128]{1,0:T(8,128)} %param.8) | copy-start | bytes 18436
Sparse Core Ops, SparseCore 0:
  144.1 106.0 all-reduce.1

commit v2 on v0

--- a/solution.py
+++ b/solution.py
@@ -17,7 +17,9 @@
         up_weight,
         preferred_element_type=jnp.float32,
     )
-    summed = lax.psum(partial_pre, "dp")
+    summed = partial_pre
+    for hop in (1, 2, 4):
+        summed = summed + lax.ppermute(summed, "dp", [(dev, dev ^ hop) for dev in range(8)])
     hidden = (jnp.maximum(summed + up_bias[None], 0.0) * cluster_mask[:, :, None]).astype(
         jnp.bfloat16
     )

time: 288 us -> 485 us (1.68)
  waiting for transfers between devices: 170 us -> 363 us
  blocking collectives: 83.4 us -> 76.8 us
  starting transfers between devices: 0.04 us -> 6.16 us
    ppermute x0 -> x3, waiting for transfers between devices: none -> 282 us  [on_device(): lax.ppermute(summed, 'dp', [(dev, dev ^ hop) for dev in range(8)])]
    psum x1 -> x0, waiting for transfers between devices: 88.9 us -> none  [on_device(): summed = lax.psum(partial_pre, 'dp')]
    all_to_all x1, blocking collectives: 83.4 us -> 76.8 us  [on_device(): lax.all_to_all(produced, 'clus', split_axis=0, concat_axis=0, tiled=True)]
    ppermute x0 -> x3, starting transfers between devices: none -> 6.15 us  [on_device(): lax.ppermute(summed, 'dp', [(dev, dev ^ hop) for dev in range(8)])]
  transfers between devices with their start and end apart: 2 -> 4, of which waited for: 2 -> 4; matrix products, arithmetic and copies ran while one was open for 0% -> 0% of each run, Pallas kernels for 0% -> 0%
where the time goes in v2:
time: 485 us; the launch traced here: 482 us
  waiting for transfers between devices  363 us (75%)
  blocking collectives  76.8 us (16%)
  matrix products  17.4 us (4%)
  between operations  13.4 us (3%)
  starting transfers between devices  6.16 us (1%)
  other arithmetic  5.42 us (1%)
    ppermute x3, waiting for transfers between devices, on_device(): lax.ppermute(summed, 'dp', [(dev, dev ^ hop) for dev in range(8)])  282 us
    all_gather x1, waiting for transfers between devices, on_device(): lax.all_gather(activations, 'clus', axis=0, tiled=True)  80.6 us
    all_to_all x1, blocking collectives, on_device(): lax.all_to_all(produced, 'clus', split_axis=0, concat_axis=0, tiled=True)  76.8 us
  transfers between devices with their start and end apart: 4, of which 4 were waited for; matrix products, arithmetic and copies ran while one was open for 0% of the time, Pallas kernels for 0%

profile of v2, /device:TPU:19, one launch (start us, length us, event | category | flops | bytes accessed | tf_op | source)
XLA Modules:
  0.0 482.2 jit_solution(11523214223139447040)
XLA Ops:
  6.5 0.0 all-gather.2.cloned.1.call-start
  6.5 0.7 all-gather.2.cloned.1.call-update
  7.3 80.6 %all-gather.2.cloned.1.call-done = bf16[1024,1536]{1,0:T(8,128)(2,1)} async-done(((bf16[32,1536]{1,0:T(8,128)(2,1)}), bf16[1024,1536]{1,0:T(8,128)(2,1)}) %all-gather.2.cloned.1.call-update) | async-done | bytes 3145744 | tf_op jit(solution)/shard_map/all_gather | solution.py:16
  87.9 7.8 %fusion = f32[1024,12,128]{2,0,1:T(8,128)S(1)} fusion(bf16[12,1536,128]{2,1,0:T(8,128)(2,1)} %param.7, bf16[1024,1536]{1,0:T(8,128)(2,1)} %all-gather.2.cloned.1.call-done), kind=kOutput, calls=%fused_computation.2 | convolution fusion | flops 4831838208 | bytes 14155776 | tf_op jit(solution)/shard_map/rd,cdn->rcn/dot_general | solution.py:14
  95.7 4.0 collective-permute-start
  99.7 9.8 %collective-permute-done = f32[1024,12,128]{2,0,1:T(8,128)S(1)} collective-permute-done((f32[1024,12,128]{2,0,1:T(8,128)S(1)}, f32[1024,12,128]{2,0,1:T(8,128)S(1)}, u32[]{:S(2)}, u32[]{:S(2)}) %collective-permute-start) | collective-permute-done | bytes 6291488 | tf_op jit(solution)/shard_map/ppermute | solution.py:22
  109.5 0.6 add.27
  110.2 0.0 copy-start
  110.2 0.0 copy-start.1
  110.2 0.4 collective-permute-start.1
  110.5 136.5 %collective-permute-done.1 = f32[1024,12,128]{2,0,1:T(8,128)S(1)} collective-permute-done((f32[1024,12,128]{2,0,1:T(8,128)S(1)}, f32[1024,12,128]{2,0,1:T(8,128)S(1)}, u32[]{:S(2)}, u32[]{:S(2)}) %collective-permute-start.1) | collective-permute-done | bytes 6291488 | tf_op jit(solution)/shard_map/ppermute | solution.py:22
  247.0 3.3 add.28
  250.3 1.8 collective-permute-start.2
  252.1 0.0 copy-done
  252.1 0.4 compare_reduce_fusion
  252.5 135.4 %collective-permute-done.2 = f32[1024,12,128]{2,0,1:T(8,128)} collective-permute-done((f32[1024,12,128]{2,0,1:T(8,128)}, f32[1024,12,128]{2,0,1:T(8,128)}, u32[]{:S(2)}, u32[]{:S(2)}) %collective-permute-start.2) | collective-permute-done | bytes 6291488 | tf_op jit(solution)/shard_map/ppermute | solution.py:22
  387.9 0.0 copy-done.1
  387.9 9.6 %bitcast_convert_fusion = bf16[1024,1536]{1,0:T(8,128)(2,1)S(1)} fusion(bf16[12,128,1536]{2,1,0:T(8,128)(2,1)} %param.9, f32[1024,12,128]{2,0,1:T(8,128)} %add.28, f32[1024,12,128]{2,0,1:T(8,128)} %collective-permute-done.2, f32[1024,12]{0,1:T(8,128)S(1)} %convert_element_type.15, f32[12,128]{1,0:T(8,128)S(1)} %copy-done.1), kind=kOutput, calls=%fused_computation | convolution fusion | flops 4841275392 | bytes 20502528 | tf_op jit(solution)/shard_map/rcn,cnd->rd/dot_general | solution.py:26
  397.5 76.8 %all_to_all.9 = bf16[32,32,1536]{2,1,0:T(8,128)(2,1)S(1)} all-to-all(bf16[32,32,1536]{2,1,0:T(8,128)(2,1)S(1)} %bitcast.8), channel_id=1, replica_groups=mesh['dp'=8,'clus'=32] {'clus'}, dimensions={0} | all-to-all | bytes 6291456 | tf_op jit(solution)/shard_map/all_to_all | solution.py:29
  474.3 1.1 reduce_sum.12
  (2 shorter events, 0.0 us)
Async XLA Ops:
  6.5 81.4 %all-gather.2.cloned.1.call-start = ((), (), s32[]{:S(2)}) async-start(), calls=%async_computation.1 | async-start | bytes 3244032 | tf_op jit(solution)/shard_map/all_gather | solution.py:16
  95.7 13.8 %collective-permute-start = (f32[1024,12,128]{2,0,1:T(8,128)S(1)}, f32[1024,12,128]{2,0,1:T(8,128)S(1)}, u32[]{:S(2)}, u32[]{:S(2)}) collective-permute-start(f32[1024,12,128]{2,0,1:T(8,128)S(1)} %fusion), channel_id=1, source_target_pairs={{0,32},{32,0},{64,96},{96,64},{128,160},{160,128},{192,224},{224,1... | collective-permute-start | bytes 18874376 | tf_op jit(solution)/shard_map/ppermute | solution.py:22
  110.2 141.9 %copy-start = (s32[1024,48]{0,1:T(8,128)S(1)}, s32[1024,48]{0,1:T(8,128)}, u32[]{:S(2)}) copy-start(s32[1024,48]{0,1:T(8,128)} %param.6) | copy-start | bytes 589828
  110.2 277.7 %copy-start.1 = (f32[12,128]{1,0:T(8,128)S(1)}, f32[12,128]{1,0:T(8,128)}, u32[]{:S(2)}) copy-start(f32[12,128]{1,0:T(8,128)} %param.8) | copy-start | bytes 18436
  110.2 136.8 %collective-permute-start.1 = (f32[1024,12,128]{2,0,1:T(8,128)S(1)}, f32[1024,12,128]{2,0,1:T(8,128)S(1)}, u32[]{:S(2)}, u32[]{:S(2)}) collective-permute-start(f32[1024,12,128]{2,0,1:T(8,128)S(1)} %add.27), channel_id=1, source_target_pairs={{0,64},{32,96},{64,0},{96,32},{128,192},{160,224},{192,128},{224,1... | collective-permute-start | bytes 18874376 | tf_op jit(solution)/shard_map/ppermute | solution.py:22
  250.3 137.6 %collective-permute-start.2 = (f32[1024,12,128]{2,0,1:T(8,128)}, f32[1024,12,128]{2,0,1:T(8,128)}, u32[]{:S(2)}, u32[]{:S(2)}) collective-permute-start(f32[1024,12,128]{2,0,1:T(8,128)} %add.28), channel_id=1, source_target_pairs={{0,128},{32,160},{64,192},{96,224},{128,0},{160,32},{192,64},{224,... | collective-permute-start | bytes 18874376 | tf_op jit(solution)/shard_map/ppermute | solution.py:22
Sparse Core Ops, SparseCore 0:
  9.9 77.9 all-gather.1
